TPU v7x, 32 devices: a whole 2x2x4 slice. The times are simulated.
32 devices in a mesh: rep: 2 (over y), seq: 4 (over z), head: 4 (over x, core).
Axes of the slice: x: 2, y: 2, z: 4, core: 2. Of those that a mesh axis runs over, the one named last changes fastest.
Arguments:
- queries: bfloat16 [4096, 1024], P(('rep', 'seq', 'head')), parts along dimension 0, may hold values from -6 to 6
- keys: bfloat16 [4096, 2, 1024], P(('rep', 'seq', 'head')), parts along dimension 0, may hold values from -6 to 6
- values: bfloat16 [4096, 2, 1024], P(('rep', 'seq', 'head')), parts along dimension 0, may hold values from -6 to 6
- out_gate: bfloat16 [4096, 1024], P(('rep', 'seq', 'head')), parts along dimension 0, may hold values from -6 to 6
- write_rate: bfloat16 [4096, 2, 8], P(('rep', 'seq', 'head')), parts along dimension 0, may hold values from 0 to 2
- log_decay: bfloat16 [4096, 8], P(('rep', 'seq', 'head')), parts along dimension 0, may hold values from -0.7 to 0
- doc_starts: int32 [8], P('rep'), parts along dimension 0, may hold values from 0 to 2047, as said below
- norm_gain: float32 [128], replicated, may hold values from 0.1 to 1.9
- out_weight: bfloat16 [1024, 2048], P(None, 'head'), may hold values from -0.1875 to 0.1875
Outputs:
- layer_out: bfloat16 [4096, 2048], P(('rep', 'seq'), 'head'), parts along dimension 0
There are 2 independent parts, one for each index of `rep`. A program takes and returns all parts, laid end to end along the dimension named above; an argument that names none is the same for every part. Nothing has to cross between parts.
Inputs may be any that keep to these rules, and one draw needn't show every extreme that they name: `doc_starts`: rises strictly from 0; one document holds exactly 1024 tokens, every other fewer, each at least one.
All inputs are finite; a program needn't handle non-finite values.
Results may differ from a plain program's by a relative error of at most 0.007.
Values may be sent and summed in bfloat16 or wider, within the bound.
A program may use at most 64 MiB of HBM per device.

v0:
```python
import math
import jax
import jax.numpy as jnp
from jax import lax
from jax.sharding import PartitionSpec as P

PRECISE_SETTING = lax.Precision.HIGHEST


def passed_along(value, axis, steps):
    count = lax.axis_size(axis)
    initial, last = (max(0, -steps), min(count, count - steps))
    return lax.ppermute(value, axis, [(source, source + steps) for source in range(initial, last)])


def doc_index(token_position, doc_starts):
    return jnp.sum((token_position[:, None] >= doc_starts[None, :]).astype(jnp.int32), 1) - 1


def advance(carry_pair, step_pair):
    current_state, through_map = carry_pair
    step_map, step_add = step_pair
    new_state = (
        jnp.einsum("hde,hef->hdf", step_map, current_state, precision=PRECISE_SETTING) + step_add
    )
    new_map = jnp.einsum("hde,hef->hdf", step_map, through_map, precision=PRECISE_SETTING)
    return ((new_state, new_map), (current_state, through_map))


def stretch_pieces(
    query_part,
    key_part,
    value_part,
    rate_part,
    decay_part,
    first_pos,
    doc_starts,
    heads_here,
    head_depth,
):
    group_len = query_part.shape[0]
    steps_len = 2 * group_len
    block_len = math.gcd(128, steps_len)
    block_count = steps_len // block_len
    half_len = block_len // 2
    read_rows = (
        query_part.reshape(group_len, heads_here, head_depth).astype(jnp.float32).transpose(1, 0, 2)
    )
    read_rows = read_rows.reshape(heads_here, block_count, half_len, head_depth)
    key_rows = key_part.reshape(group_len, 2, heads_here, head_depth).astype(jnp.float32)
    key_rows = key_rows / jnp.sqrt(jnp.sum(key_rows * key_rows, -1, keepdims=True) + 1e-06)
    key_rows = key_rows.transpose(2, 0, 1, 3).reshape(
        heads_here, block_count, block_len, head_depth
    )
    value_rows = value_part.reshape(group_len, 2, heads_here, head_depth).astype(jnp.float32)
    value_rows = value_rows.transpose(2, 0, 1, 3).reshape(
        heads_here, block_count, block_len, head_depth
    )
    rate_rows = (
        rate_part.astype(jnp.float32).transpose(2, 0, 1).reshape(heads_here, block_count, block_len)
    )
    decay_logs = decay_part.reshape(group_len, heads_here).astype(jnp.float32)
    decay_logs = jnp.stack([decay_logs, jnp.zeros_like(decay_logs)], 1).transpose(2, 0, 1)
    totals = jnp.cumsum(decay_logs.reshape(heads_here, block_count, block_len), -1)
    doc_ids = doc_index(first_pos + jnp.arange(group_len, dtype=jnp.int32), doc_starts)
    doc_before = doc_index(jnp.reshape(first_pos - 1, (1,)), doc_starts)
    step_docs = jnp.repeat(doc_ids, 2).reshape(block_count, block_len)
    prior_docs = jnp.concatenate([doc_before, step_docs[:-1, -1]])
    step_index = jnp.arange(block_len)
    within = step_index[:, None] >= step_index[None, :]
    strict = step_index[:, None] > step_index[None, :]
    same_doc = step_docs[:, :, None] == step_docs[:, None, :]
    causal_doc = within & same_doc
    spread = totals[..., :, None] - totals[..., None, :]
    decay_ratio = jnp.where(causal_doc, jnp.exp(jnp.where(causal_doc, spread, 0.0)), 0.0)
    start_gain = jnp.where(step_docs == prior_docs[:, None], jnp.exp(totals), 0.0)
    end_gain = jnp.where(step_docs == step_docs[:, -1:], jnp.exp(totals[..., -1:] - totals), 0.0)
    key_gram = jnp.einsum("hcid,hcjd->hcij", key_rows, key_rows, precision=PRECISE_SETTING)
    lower_part = jnp.where(strict, rate_rows[..., :, None] * decay_ratio * key_gram, 0.0)
    system = lower_part + jnp.eye(block_len, dtype=jnp.float32)
    right_side = jnp.concatenate(
        [rate_rows[..., None] * value_rows, (rate_rows * start_gain)[..., None] * key_rows], -1
    )
    solved = jax.scipy.linalg.solve_triangular(system, right_side, lower=True, unit_diagonal=True)
    written = solved[..., :head_depth]
    erased = solved[..., head_depth:]
    scores = (
        jnp.einsum("hcrd,hcjd->hcrj", read_rows, key_rows, precision=PRECISE_SETTING)
        * decay_ratio[:, :, 1::2, :]
    )
    inner_out = jnp.einsum("hcrj,hcje->hcre", scores, written, precision=PRECISE_SETTING)
    carried = start_gain[:, :, 1::2, None] * read_rows - jnp.einsum(
        "hcrj,hcje->hcre", scores, erased, precision=PRECISE_SETTING
    )
    weighted = end_gain[..., None] * key_rows
    identity_map = jnp.broadcast_to(
        jnp.eye(head_depth, dtype=jnp.float32), (heads_here, head_depth, head_depth)
    )
    transition = start_gain[..., -1, None, None] * identity_map[:, None] - jnp.einsum(
        "hcid,hcie->hcde", weighted, erased, precision=PRECISE_SETTING
    )
    fresh_state = jnp.einsum("hcid,hcie->hcde", weighted, written, precision=PRECISE_SETTING)
    zero_state = jnp.zeros((heads_here, head_depth, head_depth), jnp.float32)
    ends_pair, starts_pair = lax.scan(
        advance,
        (zero_state, identity_map),
        (transition.transpose(1, 0, 2, 3), fresh_state.transpose(1, 0, 2, 3)),
    )
    local_end, local_map = ends_pair
    block_starts, block_maps = starts_pair
    return (inner_out, carried, block_starts, block_maps, local_end, local_map)


def finish_readout(inner_out, carried, block_starts, block_maps, incoming):
    heads_here = inner_out.shape[0]
    head_depth = inner_out.shape[-1]
    begin_state = block_starts + jnp.einsum(
        "chde,hef->chdf", block_maps, incoming, precision=PRECISE_SETTING
    )
    readout = inner_out + jnp.einsum(
        "hcrd,chde->hcre", carried, begin_state, precision=PRECISE_SETTING
    )
    return readout.reshape(heads_here, -1, head_depth).transpose(1, 0, 2)


def norm_rows(readout, gate_part, norm_gain):
    group_len, heads_here, head_depth = readout.shape
    gate_vals = gate_part.reshape(group_len, heads_here, head_depth).astype(jnp.float32)
    inv_rms = lax.rsqrt(jnp.mean(readout * readout, -1, keepdims=True) + 1e-05)
    normed = (readout * inv_rms * norm_gain * jax.nn.silu(gate_vals)).astype(jnp.bfloat16)
    return normed.reshape(group_len, heads_here * head_depth)


def chain_states(local_map, local_end):
    heads_here, head_depth = (local_map.shape[0], local_map.shape[1])
    zero_state = jnp.zeros((heads_here, head_depth, head_depth), jnp.float32)

    def relay_once(turn_index, incoming):
        outgoing = (
            jnp.einsum("hde,hef->hdf", local_map, incoming, precision=PRECISE_SETTING) + local_end
        )
        return passed_along(outgoing.astype(jnp.bfloat16), "seq", 1).astype(outgoing.dtype)

    incoming = lax.fori_loop(0, lax.axis_size("seq") - 1, relay_once, zero_state)
    return incoming


def on_device(
    queries, keys, values, out_gate, write_rate, log_decay, doc_starts, norm_gain, out_weight
):
    tok_dev, feature_width = queries.shape
    heads_all = log_decay.shape[1]
    groups = lax.axis_size("head")
    local_heads = heads_all // groups
    head_depth = feature_width // heads_all
    arrived = (
        lax.all_to_all(queries[:, None, :], "head", split_axis=2, concat_axis=0, tiled=True),
        lax.all_to_all(keys, "head", split_axis=2, concat_axis=0, tiled=True),
        lax.all_to_all(values, "head", split_axis=2, concat_axis=0, tiled=True),
        lax.all_to_all(out_gate[:, None, :], "head", split_axis=2, concat_axis=0, tiled=True),
        lax.all_to_all(write_rate, "head", split_axis=2, concat_axis=0, tiled=True),
        lax.all_to_all(log_decay[:, None, :], "head", split_axis=2, concat_axis=0, tiled=True),
    )
    query_part, key_part, value_part, gate_part, rate_part, decay_part = arrived
    group_len = query_part.shape[0]
    first_pos = lax.axis_index("seq") * group_len
    inner_out, carried, block_starts, block_maps, local_end, local_map = stretch_pieces(
        query_part,
        key_part,
        value_part,
        rate_part,
        decay_part,
        first_pos,
        doc_starts,
        local_heads,
        head_depth,
    )
    incoming = chain_states(local_map, local_end)
    readout = finish_readout(inner_out, carried, block_starts, block_maps, incoming)
    normed = norm_rows(readout, gate_part, norm_gain)
    acc_total = jnp.dot(
        lax.all_gather(normed, "head", axis=1, tiled=True),
        out_weight,
        preferred_element_type=jnp.float32,
    )
    return acc_total.astype(jnp.bfloat16)


def solution(mesh):
    placed = (
        P(("rep", "seq", "head"), None),
        P(("rep", "seq", "head"), None, None),
        P(("rep", "seq", "head"), None, None),
        P(("rep", "seq", "head"), None),
        P(("rep", "seq", "head"), None, None),
        P(("rep", "seq", "head"), None),
        P("rep"),
        P(),
        P(None, "head"),
    )
    return jax.shard_map(
        on_device, mesh=mesh, in_specs=placed, out_specs=P(("rep", "seq"), "head"), check_vma=False
    )
```

profile of v0, /device:TPU:0, one launch (start us, length us, event | category | flops | bytes accessed | tf_op | source)
XLA Modules:
  0.0 342.5 jit_solution(240848373415669369)
XLA Ops:
  8.0 4.2 %all-to-all-start.2 = ((bf16[4,2,128]{2,1,0:T(2,128)(2,1)}), bf16[4,2,128]{2,1,0:T(2,128)(2,1)S(1)}, u32[]{:S(2)}, u32[]{:S(2)}) async-start(bf16[4,2,128]{2,1,0:T(2,128)(2,1)} %bitcast.133), calls=%async_computation.2 | async-start | bytes 4096 | tf_op jit(solution)/shard_map/all_to_all | solution.py:162
  31.4 3.3 all-to-all-start.3
  35.8 2.7 all-to-all-done.3
  38.5 3.4 all-to-all-start.1
  43.9 4.0 %all-to-all-done.1 = bf16[4,2,16384]{2,1,0:T(2,128)(2,1)S(1)} async-done(((bf16[4,2,16384]{2,1,0:T(2,128)(2,1)}), bf16[4,2,16384]{2,1,0:T(2,128)(2,1)S(1)}, u32[]{:S(2)}, u32[]{:S(2)}) %all-to-all-start.1) | async-done | bytes 262176 | tf_op jit(solution)/shard_map/all_to_all | solution.py:157
  47.9 3.4 all-to-all-start.5
  51.9 5.5 %all-to-all-done.5 = bf16[4,2,16384]{2,1,0:T(2,128)(2,1)S(1)} async-done(((bf16[4,2,16384]{2,1,0:T(2,128)(2,1)}), bf16[4,2,16384]{2,1,0:T(2,128)(2,1)S(1)}, u32[]{:S(2)}, u32[]{:S(2)}) %all-to-all-start.5) | async-done | bytes 262176 | tf_op jit(solution)/shard_map/all_to_all | solution.py:160
  57.3 3.5 %all-to-all-start = ((bf16[128,2,1024]{0,1,2:T(2,128)(2,1)}), bf16[128,2,1024]{0,1,2:T(2,128)(2,1)S(1)}, u32[]{:S(2)}, u32[]{:S(2)}) async-start(bf16[128,2,1024]{0,1,2:T(2,128)(2,1)} %copy.164), calls=%async_computation | async-start | bytes 1048576 | tf_op jit(solution)/shard_map/all_to_all | solution.py:158
  66.3 3.3 all-to-all-done
  69.6 4.1 %all-to-all-start.4 = ((bf16[128,2,1024]{0,1,2:T(2,128)(2,1)}), bf16[128,2,1024]{0,1,2:T(2,128)(2,1)}, u32[]{:S(2)}, u32[]{:S(2)}) async-start(bf16[128,2,1024]{0,1,2:T(2,128)(2,1)} %copy.177), calls=%async_computation.4 | async-start | bytes 1048576 | tf_op jit(solution)/shard_map/all_to_all | solution.py:159
  78.5 4.2 %all-to-all-done.4 = bf16[128,2,1024]{0,1,2:T(2,128)(2,1)} async-done(((bf16[128,2,1024]{0,1,2:T(2,128)(2,1)}), bf16[128,2,1024]{0,1,2:T(2,128)(2,1)}, u32[]{:S(2)}, u32[]{:S(2)}) %all-to-all-start.4) | async-done | bytes 524320 | tf_op jit(solution)/shard_map/all_to_all | solution.py:159
  85.6 3.0 copy.179
  88.7 3.4 %fusion.26 = f32[2,8,1,128,128]{4,3,2,1,0:T(8,128)} fusion(f32[2,8,128,128]{3,2,1,0:T(8,128)S(1)} %bitcast.148, f32[128,128]{1,0:T(8,128)S(1)} %copy-done.16, f32[128,128]{1,0:T(8,128)S(1)} %copy-done.7, f32[2,8,128]{2,1,0:T(8,128)S(1)} %copy-done.15, pred[128,128]{1,0:T(8,128)(4,1)S(1)} %copy-done.19, pred[128,128]{1,0:T(8,128)(4,1)S(1)} %copy-done.20, ...), kind=kOutput, calls=%fused_computation.35 | convolution fusion | flops 405012480 | bytes 2408448 | tf_op jit(solution)/shard_map/hcid,hcjd->hcij/dot_general | solution.py:78
  92.2 158.6 %custom-call.4 = f32[2,8,1,128,128]{3,4,2,1,0:T(8,128)} custom-call(f32[2,8,1,128,128]{4,3,2,1,0:T(8,128)} %fusion.26), custom_call_target="InvertDiagBlocksLowerTriangular" | custom-call | tf_op jit(solution)/shard_map/jit(_solve_triangular)/vmap(vmap())/triangular_solve | solution.py:84
  250.8 2.3 fusion.27
  260.2 3.2 convolution_bitcast_fusion.1
  265.7 23.6 %while.28 = (s32[]{:T(128)}, f32[2,128,128]{2,1,0:T(8,128)S(1)}, f32[2,128,128]{2,1,0:T(8,128)S(1)}, f32[8,2,128,128]{2,3,1,0:T(8,128)}, f32[8,2,128,128]{3,2,1,...) while((s32[]{:T(128)}, f32[2,128,128]{2,1,0:T(8,128)S(1)}, ...), condition=%wide.region_5.6_spmd.clone, body=%wide.region_4.5_spmd.clone.sunk | while | flops 100761600 | bytes 2492027 | solution.py:104
  289.3 19.3 %while.29 = (s32[]{:T(128)}, f32[2,128,128]{2,1,0:T(8,128)S(1)}, f32[2,128,128]{2,1,0:T(8,128)S(1)}, f32[2,128,128]{2,1,0:T(8,128)S(1)}, s32[]{:T(128)}, /*index=5*/s32[]{:T(128)}) while((s32[]{:T(128)}, f32[2,128,128]{2,1,0:T(8,128)S(1)}, f32[2,128,128]{2,1,0:T(8,128)S(1)}, f32[2,128,128]{2,1,0:T(8,128)S(1)}, s32[]{:T(128)}, ...), condition=%wide.region_7.8_spmd.clone, body=%wide.region_6.7_spmd.clone.sunk | while | flops 50462720 | bytes 917623 | solution.py:144
  289.6 3.9 %collective-permute-start = (bf16[2,128,128]{2,1,0:T(8,128)(2,1)S(1)}, bf16[2,128,128]{2,1,0:T(8,128)(2,1)S(1)}, u32[]{:S(2)}, u32[]{:S(2)}) collective-permute-start(bf16[2,128,128]{2,1,0:T(8,128)(2,1)S(1)} %fusion.76), channel_id=1, source_target_pairs={{0,4},{4,8},{8,12},{1,5},{5,9},{9,13},{2,6},{6,10},{10,14},{3,7},{... | collective-permute-start | bytes 196616 | tf_op jit(solution)/shard_map/while/body/eval_jaxpr/ppermute | solution.py:13
  295.8 4.3 %collective-permute-start = (bf16[2,128,128]{2,1,0:T(8,128)(2,1)S(1)}, bf16[2,128,128]{2,1,0:T(8,128)(2,1)S(1)}, u32[]{:S(2)}, u32[]{:S(2)}) collective-permute-start(bf16[2,128,128]{2,1,0:T(8,128)(2,1)S(1)} %fusion.76), channel_id=1, source_target_pairs={{0,4},{4,8},{8,12},{1,5},{5,9},{9,13},{2,6},{6,10},{10,14},{3,7},{... | collective-permute-start | bytes 196616 | tf_op jit(solution)/shard_map/while/body/eval_jaxpr/ppermute | solution.py:13
  302.2 4.3 %collective-permute-start = (bf16[2,128,128]{2,1,0:T(8,128)(2,1)S(1)}, bf16[2,128,128]{2,1,0:T(8,128)(2,1)S(1)}, u32[]{:S(2)}, u32[]{:S(2)}) collective-permute-start(bf16[2,128,128]{2,1,0:T(8,128)(2,1)S(1)} %fusion.76), channel_id=1, source_target_pairs={{0,4},{4,8},{8,12},{1,5},{5,9},{9,13},{2,6},{6,10},{10,14},{3,7},{... | collective-permute-start | bytes 196616 | tf_op jit(solution)/shard_map/while/body/eval_jaxpr/ppermute | solution.py:13
  308.7 2.7 fusion.20
  314.9 18.0 %all-gather.2.cloned.1.call-done = bf16[512,1024]{0,1:T(8,128)(2,1)} async-done(((bf16[512,256]{0,1:T(8,128)(2,1)}), bf16[512,1024]{0,1:T(8,128)(2,1)}) %all-gather.2.cloned.1.call-update) | async-done | bytes 1048592 | tf_op jit(solution)/shard_map/all_gather | solution.py:182
  332.9 2.8 convolution_convert_fusion
  (204 shorter events, 78.9 us)
Async XLA Ops:
  6.5 326.4 %copy-start = (bf16[1024,512]{1,0:T(8,128)(2,1)S(1)}, bf16[1024,512]{1,0:T(8,128)(2,1)}, u32[]{:S(2)}) copy-start(bf16[1024,512]{1,0:T(8,128)(2,1)} %param.21) | copy-start | bytes 3145732
  6.5 17.8 %copy-start.11 = (bf16[128,2,1024]{2,1,0:T(2,128)(2,1)S(1)}, bf16[128,2,1024]{2,1,0:T(2,128)(2,1)}, u32[]{:S(2)}) copy-start(bf16[128,2,1024]{2,1,0:T(2,128)(2,1)} %param.14) | copy-start | bytes 1572868
  6.5 19.7 %copy-start.12 = (bf16[128,2,1024]{2,1,0:T(2,128)(2,1)S(1)}, bf16[128,2,1024]{2,1,0:T(2,128)(2,1)}, u32[]{:S(2)}) copy-start(bf16[128,2,1024]{2,1,0:T(2,128)(2,1)} %param.15) | copy-start | bytes 1572868
  8.0 23.5 %all-to-all-start.2 = ((bf16[4,2,128]{2,1,0:T(2,128)(2,1)}), bf16[4,2,128]{2,1,0:T(2,128)(2,1)S(1)}, u32[]{:S(2)}, u32[]{:S(2)}) async-start(bf16[4,2,128]{2,1,0:T(2,128)(2,1)} %bitcast.133), calls=%async_computation.2 | async-start | bytes 4096 | tf_op jit(solution)/shard_map/all_to_all | solution.py:162
  16.9 25.1 %copy-start.9 = (pred[8,128,128]{2,1,0:T(8,128)(4,1)}, pred[8,128,128]{2,1,0:T(8,128)(4,1)S(1)}, u32[]{:S(2)}) copy-start(pred[8,128,128]{2,1,0:T(8,128)(4,1)S(1)} %compare_and_fusion) | copy-start | bytes 393220
  19.5 8.6 %copy-start.13 = (bf16[128,1024]{1,0:T(8,128)(2,1)S(1)}, bf16[128,1024]{1,0:T(8,128)(2,1)}, u32[]{:S(2)}) copy-start(bf16[128,1024]{1,0:T(8,128)(2,1)} %param.16) | copy-start | bytes 786436
  31.4 7.1 %all-to-all-start.3 = ((bf16[128,2,8]{0,1,2:T(2,128)(2,1)}), bf16[128,2,8]{0,1,2:T(2,128)(2,1)S(1)}, u32[]{:S(2)}, u32[]{:S(2)}) async-start(bf16[128,2,8]{0,1,2:T(2,128)(2,1)} %copy.175), calls=%async_computation.3 | async-start | bytes 8192 | tf_op jit(solution)/shard_map/all_to_all | solution.py:161
  38.5 9.4 %all-to-all-start.1 = ((bf16[4,2,16384]{2,1,0:T(2,128)(2,1)}), bf16[4,2,16384]{2,1,0:T(2,128)(2,1)S(1)}, u32[]{:S(2)}, u32[]{:S(2)}) async-start(bf16[4,2,16384]{2,1,0:T(2,128)(2,1)} %reshape.194), calls=%async_computation.1 | async-start | bytes 524288 | tf_op jit(solution)/shard_map/all_to_all | solution.py:157
  42.3 18.5 %copy-start.22 = (pred[8,128]{1,0:T(8,128)(4,1)S(1)}, pred[8,128]{1,0:T(8,128)(4,1)}, u32[]{:S(2)}) copy-start(pred[8,128]{1,0:T(8,128)(4,1)} %copy.182) | copy-start | bytes 3076
  42.3 18.5 %copy-start.23 = (pred[8,128]{1,0:T(8,128)(4,1)S(1)}, pred[8,128]{1,0:T(8,128)(4,1)}, u32[]{:S(2)}) copy-start(pred[8,128]{1,0:T(8,128)(4,1)} %copy.180) | copy-start | bytes 3076
  47.9 9.4 %all-to-all-start.5 = ((bf16[4,2,16384]{2,1,0:T(2,128)(2,1)}), bf16[4,2,16384]{2,1,0:T(2,128)(2,1)S(1)}, u32[]{:S(2)}, u32[]{:S(2)}) async-start(bf16[4,2,16384]{2,1,0:T(2,128)(2,1)} %reshape.196), calls=%async_computation.5 | async-start | bytes 524288 | tf_op jit(solution)/shard_map/all_to_all | solution.py:160
  51.8 11.4 %copy-start.14 = (f32[2,8,128]{2,1,0:T(8,128)}, f32[2,8,128]{2,1,0:T(8,128)S(1)}, u32[]{:S(2)}) copy-start(f32[2,8,128]{2,1,0:T(8,128)S(1)} %reshape.172) | copy-start | bytes 24580
  57.3 12.3 %all-to-all-start = ((bf16[128,2,1024]{0,1,2:T(2,128)(2,1)}), bf16[128,2,1024]{0,1,2:T(2,128)(2,1)S(1)}, u32[]{:S(2)}, u32[]{:S(2)}) async-start(bf16[128,2,1024]{0,1,2:T(2,128)(2,1)} %copy.164), calls=%async_computation | async-start | bytes 1048576 | tf_op jit(solution)/shard_map/all_to_all | solution.py:158
  69.6 13.1 %all-to-all-start.4 = ((bf16[128,2,1024]{0,1,2:T(2,128)(2,1)}), bf16[128,2,1024]{0,1,2:T(2,128)(2,1)}, u32[]{:S(2)}, u32[]{:S(2)}) async-start(bf16[128,2,1024]{0,1,2:T(2,128)(2,1)} %copy.177), calls=%async_computation.4 | async-start | bytes 1048576 | tf_op jit(solution)/shard_map/all_to_all | solution.py:159
  73.8 259.1 %all-gather.2.cloned.1.call-start = ((), (), s32[]{:S(2)}) async-start(), calls=%async_computation.6 | async-start | bytes 1310720 | tf_op jit(solution)/shard_map/all_gather | solution.py:182
  84.1 4.6 %copy-start.7 = (f32[128,128]{1,0:T(8,128)S(1)}, f32[128,128]{1,0:T(8,128)}, u32[]{:S(2)}) copy-start(f32[128,128]{1,0:T(8,128)} %get-tuple-element.189) | copy-start | bytes 196612
  84.1 4.6 %copy-start.15 = (f32[2,8,128]{2,1,0:T(8,128)S(1)}, f32[2,8,128]{2,1,0:T(8,128)}, u32[]{:S(2)}) copy-start(f32[2,8,128]{2,1,0:T(8,128)} %copy-done.14) | copy-start | bytes 24580
  84.1 4.6 %copy-start.19 = (pred[128,128]{1,0:T(8,128)(4,1)S(1)}, pred[128,128]{1,0:T(8,128)(4,1)}, u32[]{:S(2)}) copy-start(pred[128,128]{1,0:T(8,128)(4,1)} %get-tuple-element.187) | copy-start | bytes 49156
  84.1 4.6 %copy-start.20 = (pred[128,128]{1,0:T(8,128)(4,1)S(1)}, pred[128,128]{1,0:T(8,128)(4,1)}, u32[]{:S(2)}) copy-start(pred[128,128]{1,0:T(8,128)(4,1)} %get-tuple-element.188) | copy-start | bytes 49156
  88.7 162.1 %copy-start.2 = (bf16[2,512,128]{2,1,0:T(8,128)(2,1)S(1)}, bf16[2,512,128]{2,1,0:T(8,128)(2,1)}, u32[]{:S(2)}) copy-start(bf16[2,512,128]{2,1,0:T(8,128)(2,1)} %copy.169) | copy-start | bytes 786436
  92.2 161.0 %copy-start.18 = (f32[2,8,128]{2,1,0:T(8,128)S(1)}, f32[2,8,128]{2,1,0:T(8,128)}, u32[]{:S(2)}) copy-start(f32[2,8,128]{2,1,0:T(8,128)} %get-tuple-element.182) | copy-start | bytes 24580
  289.6 5.8 %collective-permute-start = (bf16[2,128,128]{2,1,0:T(8,128)(2,1)S(1)}, bf16[2,128,128]{2,1,0:T(8,128)(2,1)S(1)}, u32[]{:S(2)}, u32[]{:S(2)}) collective-permute-start(bf16[2,128,128]{2,1,0:T(8,128)(2,1)S(1)} %fusion.76), channel_id=1, source_target_pairs={{0,4},{4,8},{8,12},{1,5},{5,9},{9,13},{2,6},{6,10},{10,14},{3,7},{... | collective-permute-start | bytes 196616 | tf_op jit(solution)/shard_map/while/body/eval_jaxpr/ppermute | solution.py:13
  295.8 6.2 %collective-permute-start = (bf16[2,128,128]{2,1,0:T(8,128)(2,1)S(1)}, bf16[2,128,128]{2,1,0:T(8,128)(2,1)S(1)}, u32[]{:S(2)}, u32[]{:S(2)}) collective-permute-start(bf16[2,128,128]{2,1,0:T(8,128)(2,1)S(1)} %fusion.76), channel_id=1, source_target_pairs={{0,4},{4,8},{8,12},{1,5},{5,9},{9,13},{2,6},{6,10},{10,14},{3,7},{... | collective-permute-start | bytes 196616 | tf_op jit(solution)/shard_map/while/body/eval_jaxpr/ppermute | solution.py:13
  302.2 6.2 %collective-permute-start = (bf16[2,128,128]{2,1,0:T(8,128)(2,1)S(1)}, bf16[2,128,128]{2,1,0:T(8,128)(2,1)S(1)}, u32[]{:S(2)}, u32[]{:S(2)}) collective-permute-start(bf16[2,128,128]{2,1,0:T(8,128)(2,1)S(1)} %fusion.76), channel_id=1, source_target_pairs={{0,4},{4,8},{8,12},{1,5},{5,9},{9,13},{2,6},{6,10},{10,14},{3,7},{... | collective-permute-start | bytes 196616 | tf_op jit(solution)/shard_map/while/body/eval_jaxpr/ppermute | solution.py:13
  (11 other events, 28.2 us)
Sparse Core Ops, SparseCore 0:
  315.0 17.8 all-gather.1
where the time goes:
time: 344 us; the launch traced here: 343 us
  other arithmetic  173 us (50%)
  waiting for transfers between devices  43.3 us (13%)
  local copies, waits for them, and re-layouts  39.4 us (11%)
  matrix products  36.9 us (11%)
  starting transfers between devices  34.6 us (10%)
  between operations  14.7 us (4%)
    another operation x2, other arithmetic, stretch_pieces(): jax.scipy.linalg.solve_triangular(system, right_side, lower=True, unit_di...  159 us
    all_gather x1, waiting for transfers between devices, on_device(): lax.all_gather(normed, 'head', axis=1, tiled=True)  18 us
    ppermute x3, starting transfers between devices, passed_along(): lax.ppermute(value, axis, [(source, source + steps) for source in range(i...  12.5 us
    dynamic_update_slice x24, local copies, waits for them, and re-layouts, stretch_pieces(): lax.scan(advance, (zero_state, identity_map), (transition.transpose(1, 0,...  11.3 us
    dot_general x8, matrix products, advance(): jnp.einsum('hde,hef->hdf', step_map, current_state, precision=PRECISE_SET...  9.44 us
    unnamed x62, local copies, waits for them, and re-layouts  8.95 us
  transfers between devices with their start and end apart: 10, of which 9 were waited for; matrix products, arithmetic and copies ran while one was open for 9% of the time, Pallas kernels for 0%

commit v1 on v0

--- a/solution.py
+++ b/solution.py
@@ -5,6 +5,17 @@
 from jax.sharding import PartitionSpec as P
 
 PRECISE_SETTING = lax.Precision.HIGHEST
+
+
+def _shape_panel(in_array, which_dim, inputs):
+    before, state_next = (in_array.shape[:which_dim], in_array.shape[which_dim + 1 :])
+    return jnp.moveaxis(in_array.reshape(*before, inputs, -1, *state_next), which_dim, 0)
+
+
+def connect_tails(vector, array_axis):
+    current_arr = list(vector.shape[1:])
+    current_arr[array_axis] *= vector.shape[0]
+    return jnp.moveaxis(vector, 0, array_axis).reshape(current_arr)
 
 
 def passed_along(value, axis, steps):
@@ -148,13 +159,30 @@
 def on_device(
     queries, keys, values, out_gate, write_rate, log_decay, doc_starts, norm_gain, out_weight
 ):
+
+    def use_rails(mine_x, mesh_name, sheet, piece_in):
+        met_up, arr_now = (jax.lax.psum(1, axis_name=mesh_name), jax.lax.axis_index(mesh_name))
+        kept_arr = _shape_panel(mine_x, sheet, met_up)
+        leaves = [kept_arr[arr_now]]
+        for dev_i in tuple(range(1, met_up)):
+            arr_next = kept_arr[(arr_now + dev_i) % met_up]
+            leaves.append(
+                jax.lax.ppermute(
+                    arr_next,
+                    axis_name=mesh_name,
+                    perm=[(dev, (dev + dev_i) % met_up) for dev in range(met_up)],
+                )
+            )
+        kept_arr = jnp.stack(leaves, axis=0)[(arr_now - jnp.arange(met_up)) % met_up]
+        return connect_tails(kept_arr, piece_in)
+
     tok_dev, feature_width = queries.shape
     heads_all = log_decay.shape[1]
     groups = lax.axis_size("head")
     local_heads = heads_all // groups
     head_depth = feature_width // heads_all
     arrived = (
-        lax.all_to_all(queries[:, None, :], "head", split_axis=2, concat_axis=0, tiled=True),
+        use_rails(queries[:, None, :], "head", 2, 0),
         lax.all_to_all(keys, "head", split_axis=2, concat_axis=0, tiled=True),
         lax.all_to_all(values, "head", split_axis=2, concat_axis=0, tiled=True),
         lax.all_to_all(out_gate[:, None, :], "head", split_axis=2, concat_axis=0, tiled=True),

time: 344 us -> 332 us (0.965)
  waiting for transfers between devices: 43.3 us -> 37.2 us
    all_to_all x1 -> x0, waiting for transfers between devices: 4.01 us -> none  [on_device(): lax.all_to_all(queries[:, None, :], 'head', split_axis=2, concat_axis=0,...]
    ppermute x0 -> x3, starting transfers between devices: none -> 3.66 us  [use_rails(): jax.lax.ppermute(arr_next, axis_name=mesh_name, perm=[(dev, (dev + dev_i)...]
    unnamed x62 -> x56, local copies, waits for them, and re-layouts: 8.95 us -> 8.41 us
  transfers between devices with their start and end apart: 10 -> 12, of which waited for: 9 -> 8; matrix products, arithmetic and copies ran while one was open for 9% -> 8% of each run, Pallas kernels for 0% -> 0%
where the time goes in v1:
time: 332 us
  other arithmetic  171 us (52%)
  waiting for transfers between devices  37.2 us (11%)
  matrix products  36.9 us (11%)
  local copies, waits for them, and re-layouts  36.4 us (11%)
  starting transfers between devices  34.8 us (10%)
  between operations  14.7 us (4%)
    another operation x2, other arithmetic, stretch_pieces(): jax.scipy.linalg.solve_triangular(system, right_side, lower=True, unit_di...  159 us
    all_gather x1, waiting for transfers between devices, on_device(): lax.all_gather(normed, 'head', axis=1, tiled=True)  18 us
    ppermute x3, starting transfers between devices, passed_along(): lax.ppermute(value, axis, [(source, source + steps) for source in range(i...  12.5 us
    dynamic_update_slice x24, local copies, waits for them, and re-layouts, stretch_pieces(): lax.scan(advance, (zero_state, identity_map), (transition.transpose(1, 0,...  11.4 us
    dot_general x8, matrix products, advance(): jnp.einsum('hde,hef->hdf', step_map, current_state, precision=PRECISE_SET...  9.44 us
    unnamed x56, local copies, waits for them, and re-layouts  8.41 us
  transfers between devices with their start and end apart: 12, of which 8 were waited for; matrix products, arithmetic and copies ran while one was open for 8% of the time, Pallas kernels for 0%

profile of v1, /device:TPU:0, one launch (start us, length us, event | category | flops | bytes accessed | tf_op | source)
XLA Modules:
  0.0 331.6 jit_solution(3225652230286875750)
XLA Ops:
  8.0 4.2 %all-to-all-start.1 = ((bf16[4,2,128]{2,1,0:T(2,128)(2,1)}), bf16[4,2,128]{2,1,0:T(2,128)(2,1)S(1)}, u32[]{:S(2)}, u32[]{:S(2)}) async-start(bf16[4,2,128]{2,1,0:T(2,128)(2,1)} %bitcast.131), calls=%async_computation.1 | async-start | bytes 4096 | tf_op jit(solution)/shard_map/all_to_all | solution.py:190
  27.8 2.2 reduce.6
  30.8 3.2 all-to-all-start.2
  37.8 3.4 %all-to-all-start.4 = ((bf16[4,2,16384]{2,1,0:T(2,128)(2,1)}), bf16[4,2,16384]{2,1,0:T(2,128)(2,1)S(1)}, u32[]{:S(2)}, u32[]{:S(2)}) async-start(bf16[4,2,16384]{2,1,0:T(2,128)(2,1)} %reshape.256), calls=%async_computation.4 | async-start | bytes 524288 | tf_op jit(solution)/shard_map/all_to_all | solution.py:188
  42.3 4.9 %all-to-all-done.4 = bf16[4,2,16384]{2,1,0:T(2,128)(2,1)S(1)} async-done(((bf16[4,2,16384]{2,1,0:T(2,128)(2,1)}), bf16[4,2,16384]{2,1,0:T(2,128)(2,1)S(1)}, u32[]{:S(2)}, u32[]{:S(2)}) %all-to-all-start.4) | async-done | bytes 262176 | tf_op jit(solution)/shard_map/all_to_all | solution.py:188
  47.2 3.5 %all-to-all-start = ((bf16[128,2,1024]{0,1,2:T(2,128)(2,1)}), bf16[128,2,1024]{0,1,2:T(2,128)(2,1)S(1)}, u32[]{:S(2)}, u32[]{:S(2)}) async-start(bf16[128,2,1024]{0,1,2:T(2,128)(2,1)} %copy.211), calls=%async_computation | async-start | bytes 1048576 | tf_op jit(solution)/shard_map/all_to_all | solution.py:186
  55.7 3.8 %all-to-all-done = bf16[128,2,1024]{0,1,2:T(2,128)(2,1)S(1)} async-done(((bf16[128,2,1024]{0,1,2:T(2,128)(2,1)}), bf16[128,2,1024]{0,1,2:T(2,128)(2,1)S(1)}, u32[]{:S(2)}, u32[]{:S(2)}) %all-to-all-start) | async-done | bytes 524320 | tf_op jit(solution)/shard_map/all_to_all | solution.py:186
  59.5 4.2 %all-to-all-start.3 = ((bf16[128,2,1024]{0,1,2:T(2,128)(2,1)}), bf16[128,2,1024]{0,1,2:T(2,128)(2,1)}, u32[]{:S(2)}, u32[]{:S(2)}) async-start(bf16[128,2,1024]{0,1,2:T(2,128)(2,1)} %copy.221), calls=%async_computation.3 | async-start | bytes 1048576 | tf_op jit(solution)/shard_map/all_to_all | solution.py:187
  68.4 4.2 %all-to-all-done.3 = bf16[128,2,1024]{0,1,2:T(2,128)(2,1)} async-done(((bf16[128,2,1024]{0,1,2:T(2,128)(2,1)}), bf16[128,2,1024]{0,1,2:T(2,128)(2,1)}, u32[]{:S(2)}, u32[]{:S(2)}) %all-to-all-start.3) | async-done | bytes 524320 | tf_op jit(solution)/shard_map/all_to_all | solution.py:187
  75.5 2.1 copy.223
  77.7 3.4 %fusion.26 = f32[2,8,1,128,128]{4,3,2,1,0:T(8,128)} fusion(f32[2,8,128,128]{3,2,1,0:T(8,128)S(1)} %bitcast.146, f32[128,128]{1,0:T(8,128)S(1)} %copy-done.15, f32[128,128]{1,0:T(8,128)S(1)} %copy-done.6, f32[2,8,128]{2,1,0:T(8,128)S(1)} %copy-done.14, pred[128,128]{1,0:T(8,128)(4,1)S(1)} %copy-done.18, pred[128,128]{1,0:T(8,128)(4,1)S(1)} %copy-done.19, ...), kind=kOutput, calls=%fused_computation.36 | convolution fusion | flops 405012480 | bytes 2408448 | tf_op jit(solution)/shard_map/hcid,hcjd->hcij/dot_general | solution.py:89
  81.1 158.7 %custom-call.4 = f32[2,8,1,128,128]{3,4,2,1,0:T(8,128)} custom-call(f32[2,8,1,128,128]{4,3,2,1,0:T(8,128)} %fusion.26), custom_call_target="InvertDiagBlocksLowerTriangular" | custom-call | tf_op jit(solution)/shard_map/jit(_solve_triangular)/vmap(vmap())/triangular_solve | solution.py:95
  239.8 2.3 convolution_multiply_fusion.1
  249.1 3.2 convolution_bitcast_fusion.1
  252.3 2.2 fusion.21
  254.6 23.8 %while.28 = (s32[]{:T(128)}, f32[2,128,128]{2,1,0:T(8,128)S(1)}, f32[2,128,128]{2,1,0:T(8,128)S(1)}, f32[8,2,128,128]{2,3,1,0:T(8,128)}, f32[8,2,128,128]{3,2,1,...) while((s32[]{:T(128)}, f32[2,128,128]{2,1,0:T(8,128)S(1)}, ...), condition=%wide.region_5.6_spmd.clone, body=%wide.region_4.5_spmd.clone.sunk | while | flops 100761600 | bytes 2492027 | solution.py:115
  278.4 19.4 %while.29 = (s32[]{:T(128)}, f32[2,128,128]{2,1,0:T(8,128)S(1)}, f32[2,128,128]{2,1,0:T(8,128)S(1)}, f32[2,128,128]{2,1,0:T(8,128)S(1)}, s32[]{:T(128)}, /*index=5*/s32[]{:T(128)}) while((s32[]{:T(128)}, f32[2,128,128]{2,1,0:T(8,128)S(1)}, f32[2,128,128]{2,1,0:T(8,128)S(1)}, f32[2,128,128]{2,1,0:T(8,128)S(1)}, s32[]{:T(128)}, ...), condition=%wide.region_7.8_spmd.clone, body=%wide.region_6.7_spmd.clone.sunk | while | flops 50462720 | bytes 917623 | solution.py:155
  278.7 4.0 %collective-permute-start = (bf16[2,128,128]{2,1,0:T(8,128)(2,1)S(1)}, bf16[2,128,128]{2,1,0:T(8,128)(2,1)S(1)}, u32[]{:S(2)}, u32[]{:S(2)}) collective-permute-start(bf16[2,128,128]{2,1,0:T(8,128)(2,1)S(1)} %fusion.77), channel_id=1, source_target_pairs={{0,4},{4,8},{8,12},{1,5},{5,9},{9,13},{2,6},{6,10},{10,14},{3,7},{... | collective-permute-start | bytes 196616 | tf_op jit(solution)/shard_map/while/body/eval_jaxpr/ppermute | solution.py:24
  284.8 4.3 %collective-permute-start = (bf16[2,128,128]{2,1,0:T(8,128)(2,1)S(1)}, bf16[2,128,128]{2,1,0:T(8,128)(2,1)S(1)}, u32[]{:S(2)}, u32[]{:S(2)}) collective-permute-start(bf16[2,128,128]{2,1,0:T(8,128)(2,1)S(1)} %fusion.77), channel_id=1, source_target_pairs={{0,4},{4,8},{8,12},{1,5},{5,9},{9,13},{2,6},{6,10},{10,14},{3,7},{... | collective-permute-start | bytes 196616 | tf_op jit(solution)/shard_map/while/body/eval_jaxpr/ppermute | solution.py:24
  291.3 4.3 %collective-permute-start = (bf16[2,128,128]{2,1,0:T(8,128)(2,1)S(1)}, bf16[2,128,128]{2,1,0:T(8,128)(2,1)S(1)}, u32[]{:S(2)}, u32[]{:S(2)}) collective-permute-start(bf16[2,128,128]{2,1,0:T(8,128)(2,1)S(1)} %fusion.77), channel_id=1, source_target_pairs={{0,4},{4,8},{8,12},{1,5},{5,9},{9,13},{2,6},{6,10},{10,14},{3,7},{... | collective-permute-start | bytes 196616 | tf_op jit(solution)/shard_map/while/body/eval_jaxpr/ppermute | solution.py:24
  297.8 2.7 fusion.20
  300.5 2.1 convolution_add_fusion.2
  304.0 18.0 %all-gather.2.cloned.1.call-done = bf16[512,1024]{0,1:T(8,128)(2,1)} async-done(((bf16[512,256]{0,1:T(8,128)(2,1)}), bf16[512,1024]{0,1:T(8,128)(2,1)}) %all-gather.2.cloned.1.call-update) | async-done | bytes 1048592 | tf_op jit(solution)/shard_map/all_gather | solution.py:210
  322.0 2.7 convolution_convert_fusion
  (208 shorter events, 72.6 us)
Async XLA Ops:
  6.5 315.4 %copy-start = (bf16[1024,512]{1,0:T(8,128)(2,1)S(1)}, bf16[1024,512]{1,0:T(8,128)(2,1)}, u32[]{:S(2)}) copy-start(bf16[1024,512]{1,0:T(8,128)(2,1)} %param.21) | copy-start | bytes 3145732
  6.5 15.7 %copy-start.21 = (bf16[128,2,8]{0,2,1:T(8,128)(2,1)S(1)}, bf16[128,2,8]{0,2,1:T(8,128)(2,1)}, u32[]{:S(2)}) copy-start(bf16[128,2,8]{0,2,1:T(8,128)(2,1)} %param.17) | copy-start | bytes 12292
  6.5 16.5 %copy-start.10 = (bf16[128,2,1024]{2,1,0:T(2,128)(2,1)S(1)}, bf16[128,2,1024]{2,1,0:T(2,128)(2,1)}, u32[]{:S(2)}) copy-start(bf16[128,2,1024]{2,1,0:T(2,128)(2,1)} %param.14) | copy-start | bytes 1572868
  6.5 18.5 %copy-start.11 = (bf16[128,2,1024]{2,1,0:T(2,128)(2,1)S(1)}, bf16[128,2,1024]{2,1,0:T(2,128)(2,1)}, u32[]{:S(2)}) copy-start(bf16[128,2,1024]{2,1,0:T(2,128)(2,1)} %param.15) | copy-start | bytes 1572868
  8.0 22.8 %all-to-all-start.1 = ((bf16[4,2,128]{2,1,0:T(2,128)(2,1)}), bf16[4,2,128]{2,1,0:T(2,128)(2,1)S(1)}, u32[]{:S(2)}, u32[]{:S(2)}) async-start(bf16[4,2,128]{2,1,0:T(2,128)(2,1)} %bitcast.131), calls=%async_computation.1 | async-start | bytes 4096 | tf_op jit(solution)/shard_map/all_to_all | solution.py:190
  12.2 14.7 %copy-start.12 = (bf16[128,1024]{1,0:T(8,128)(2,1)S(1)}, bf16[128,1024]{1,0:T(8,128)(2,1)}, u32[]{:S(2)}) copy-start(bf16[128,1024]{1,0:T(8,128)(2,1)} %param.16) | copy-start | bytes 786436
  13.5 38.7 %collective-permute-start.1 = (bf16[128,1,256]{2,0,1:T(8,128)(2,1)S(1)}, bf16[128,1,256]{2,0,1:T(8,128)(2,1)S(1)}, u32[]{:S(2)}, u32[]{:S(2)}) collective-permute-start(bf16[128,1,256]{2,0,1:T(8,128)(2,1)S(1)} %bitcast.171), channel_id=1, source_target_pairs={{0,1},{1,2},{2,3},{3,0},{4,5},{5,6},{6,7},{7,4},{8,9},{9,10},{10,1... | collective-permute-start | bytes 196616 | tf_op jit(solution)/shard_map/ppermute | solution.py:170
  14.2 38.0 %collective-permute-start.2 = (bf16[128,1,256]{2,0,1:T(8,128)(2,1)S(1)}, bf16[128,1,256]{2,0,1:T(8,128)(2,1)S(1)}, u32[]{:S(2)}, u32[]{:S(2)}) collective-permute-start(bf16[128,1,256]{2,0,1:T(8,128)(2,1)S(1)} %bitcast.172), channel_id=1, source_target_pairs={{0,2},{1,3},{2,0},{3,1},{4,6},{5,7},{6,4},{7,5},{8,10},{9,11},{10,... | collective-permute-start | bytes 196616 | tf_op jit(solution)/shard_map/ppermute | solution.py:170
  16.0 36.2 %collective-permute-start.3 = (bf16[128,1,256]{2,0,1:T(8,128)(2,1)S(1)}, bf16[128,1,256]{2,0,1:T(8,128)(2,1)S(1)}, u32[]{:S(2)}, u32[]{:S(2)}) collective-permute-start(bf16[128,1,256]{2,0,1:T(8,128)(2,1)S(1)} %bitcast.173), channel_id=1, source_target_pairs={{0,3},{1,0},{2,1},{3,2},{4,7},{5,4},{6,5},{7,6},{8,11},{9,8},{10,9... | collective-permute-start | bytes 196616 | tf_op jit(solution)/shard_map/ppermute | solution.py:170
  22.1 13.0 %copy-start.8 = (pred[8,128,128]{2,1,0:T(8,128)(4,1)}, pred[8,128,128]{2,1,0:T(8,128)(4,1)S(1)}, u32[]{:S(2)}) copy-start(pred[8,128,128]{2,1,0:T(8,128)(4,1)S(1)} %compare_and_fusion) | copy-start | bytes 393220
  30.8 7.0 %all-to-all-start.2 = ((bf16[128,2,8]{0,1,2:T(2,128)(2,1)}), bf16[128,2,8]{0,1,2:T(2,128)(2,1)S(1)}, u32[]{:S(2)}, u32[]{:S(2)}) async-start(bf16[128,2,8]{0,1,2:T(2,128)(2,1)} %copy.219), calls=%async_computation.2 | async-start | bytes 8192 | tf_op jit(solution)/shard_map/all_to_all | solution.py:189
  37.8 9.4 %all-to-all-start.4 = ((bf16[4,2,16384]{2,1,0:T(2,128)(2,1)}), bf16[4,2,16384]{2,1,0:T(2,128)(2,1)S(1)}, u32[]{:S(2)}, u32[]{:S(2)}) async-start(bf16[4,2,16384]{2,1,0:T(2,128)(2,1)} %reshape.256), calls=%async_computation.4 | async-start | bytes 524288 | tf_op jit(solution)/shard_map/all_to_all | solution.py:188
  41.7 12.7 %copy-start.13 = (f32[2,8,128]{2,1,0:T(8,128)}, f32[2,8,128]{2,1,0:T(8,128)S(1)}, u32[]{:S(2)}) copy-start(f32[2,8,128]{2,1,0:T(8,128)S(1)} %reshape.223) | copy-start | bytes 24580
  47.2 12.3 %all-to-all-start = ((bf16[128,2,1024]{0,1,2:T(2,128)(2,1)}), bf16[128,2,1024]{0,1,2:T(2,128)(2,1)S(1)}, u32[]{:S(2)}, u32[]{:S(2)}) async-start(bf16[128,2,1024]{0,1,2:T(2,128)(2,1)} %copy.211), calls=%async_computation | async-start | bytes 1048576 | tf_op jit(solution)/shard_map/all_to_all | solution.py:186
  59.5 13.1 %all-to-all-start.3 = ((bf16[128,2,1024]{0,1,2:T(2,128)(2,1)}), bf16[128,2,1024]{0,1,2:T(2,128)(2,1)}, u32[]{:S(2)}, u32[]{:S(2)}) async-start(bf16[128,2,1024]{0,1,2:T(2,128)(2,1)} %copy.221), calls=%async_computation.3 | async-start | bytes 1048576 | tf_op jit(solution)/shard_map/all_to_all | solution.py:187
  63.6 258.3 %all-gather.2.cloned.1.call-start = ((), (), s32[]{:S(2)}) async-start(), calls=%async_computation.5 | async-start | bytes 1310720 | tf_op jit(solution)/shard_map/all_gather | solution.py:210
  74.0 3.6 %copy-start.6 = (f32[128,128]{1,0:T(8,128)S(1)}, f32[128,128]{1,0:T(8,128)}, u32[]{:S(2)}) copy-start(f32[128,128]{1,0:T(8,128)} %get-tuple-element.200) | copy-start | bytes 196612
  74.0 3.6 %copy-start.14 = (f32[2,8,128]{2,1,0:T(8,128)S(1)}, f32[2,8,128]{2,1,0:T(8,128)}, u32[]{:S(2)}) copy-start(f32[2,8,128]{2,1,0:T(8,128)} %copy-done.13) | copy-start | bytes 24580
  74.0 3.6 %copy-start.18 = (pred[128,128]{1,0:T(8,128)(4,1)S(1)}, pred[128,128]{1,0:T(8,128)(4,1)}, u32[]{:S(2)}) copy-start(pred[128,128]{1,0:T(8,128)(4,1)} %get-tuple-element.198) | copy-start | bytes 49156
  74.0 3.6 %copy-start.19 = (pred[128,128]{1,0:T(8,128)(4,1)S(1)}, pred[128,128]{1,0:T(8,128)(4,1)}, u32[]{:S(2)}) copy-start(pred[128,128]{1,0:T(8,128)(4,1)} %get-tuple-element.199) | copy-start | bytes 49156
  81.1 160.9 %copy-start.17 = (f32[2,8,128]{2,1,0:T(8,128)S(1)}, f32[2,8,128]{2,1,0:T(8,128)}, u32[]{:S(2)}) copy-start(f32[2,8,128]{2,1,0:T(8,128)} %get-tuple-element.189) | copy-start | bytes 24580
  278.7 5.8 %collective-permute-start = (bf16[2,128,128]{2,1,0:T(8,128)(2,1)S(1)}, bf16[2,128,128]{2,1,0:T(8,128)(2,1)S(1)}, u32[]{:S(2)}, u32[]{:S(2)}) collective-permute-start(bf16[2,128,128]{2,1,0:T(8,128)(2,1)S(1)} %fusion.77), channel_id=1, source_target_pairs={{0,4},{4,8},{8,12},{1,5},{5,9},{9,13},{2,6},{6,10},{10,14},{3,7},{... | collective-permute-start | bytes 196616 | tf_op jit(solution)/shard_map/while/body/eval_jaxpr/ppermute | solution.py:24
  284.8 6.2 %collective-permute-start = (bf16[2,128,128]{2,1,0:T(8,128)(2,1)S(1)}, bf16[2,128,128]{2,1,0:T(8,128)(2,1)S(1)}, u32[]{:S(2)}, u32[]{:S(2)}) collective-permute-start(bf16[2,128,128]{2,1,0:T(8,128)(2,1)S(1)} %fusion.77), channel_id=1, source_target_pairs={{0,4},{4,8},{8,12},{1,5},{5,9},{9,13},{2,6},{6,10},{10,14},{3,7},{... | collective-permute-start | bytes 196616 | tf_op jit(solution)/shard_map/while/body/eval_jaxpr/ppermute | solution.py:24
  291.3 6.2 %collective-permute-start = (bf16[2,128,128]{2,1,0:T(8,128)(2,1)S(1)}, bf16[2,128,128]{2,1,0:T(8,128)(2,1)S(1)}, u32[]{:S(2)}, u32[]{:S(2)}) collective-permute-start(bf16[2,128,128]{2,1,0:T(8,128)(2,1)S(1)} %fusion.77), channel_id=1, source_target_pairs={{0,4},{4,8},{8,12},{1,5},{5,9},{9,13},{2,6},{6,10},{10,14},{3,7},{... | collective-permute-start | bytes 196616 | tf_op jit(solution)/shard_map/while/body/eval_jaxpr/ppermute | solution.py:24
  (11 other events, 26.0 us)
Sparse Core Ops, SparseCore 0:
  304.1 17.8 all-gather.1
